TPU v7x, 32 devices: a whole 2x2x4 slice. The times are simulated.
32 devices in a mesh: dev: 32 (over z, y, x, core).
Axes of the slice: x: 2, y: 2, z: 4, core: 2. Of those that a mesh axis runs over, the one named last changes fastest.
Arguments:
- states: float32 [188, 262144], P(None, 'dev'), may hold values from -6 to 6
- particle_mass: float32 [262144], P('dev'), may hold values from 1 to 10
- bin_index: int32 [262144], P('dev'), may hold values from 0 to 3
- cell_index: int32 [262144], P('dev'), may hold values from 0 to 255, as said below
- move_slot: int32 [262144], P('dev'), may hold values from -1 to 1023, as said below
- react_list: int32 [65536], P('dev'), may hold values from -1 to 8191, as said below
- rate_weights: bfloat16 [939, 188], replicated, may hold values from -0.4375 to 0.4375
- stoichiometry: bfloat16 [188, 939], replicated, may hold values from -0.1875 to 0.1875
- rate_scale: float32 [939], replicated, may hold values from 0.2 to 2
- jacobian_inverse: bfloat16 [4, 188, 188], replicated, may hold values from -1 to 2
- mixing_rate: float32 [8192], P('dev'), may hold values from 0.5 to 8
Outputs:
- mixed_states: float32 [188, 294912], P(None, 'dev')
- cell_means: float32 [188, 8192], P(None, 'dev')
Inputs may be any that keep to these rules, and one draw needn't show every extreme that they name: `move_slot`: on each device the entries that are not -1 are distinct. Entries below 512 never stand on device 0 and entries of 512 or more never on the last device. At most 512 particles of one device go each way, and that many go down from some device and up from some device. Every cell of every device keeps at least one staying particle. `cell_index`: for a staying particle, its cell on its own device; for a moving one, its cell on the device it moves to. `react_list`: each device lists distinct particles of its own first, then -1. A quarter of the devices list 2048 particles, the others 2048 // 4.
All inputs are finite; a program needn't handle non-finite values.
Results may differ from a plain program's by a relative error of at most 0.00089.
Values sent between devices are 32-bit elements; how exact they have to be, the bound alone decides.
A program may use at most 128 MiB of HBM per device.

v0:
```python
import functools
import math
import jax
import jax.numpy as jnp
from jax import lax
from jax.experimental import pallas as pl
from jax.experimental.pallas import tpu as pltpu
from jax.sharding import PartitionSpec as P

NEWTON = 3
CHEM_STEP = 0.5
MIX_RATE = 0.5
LANES = 128
SUB = 512
SUBS = 2
NCOL = SUB * SUBS
CHUNK = 256
LAG = 2
ROWS = 192
UNROLL = 8
LOADS = 4
F32, BF16, I32 = jnp.float32, jnp.bfloat16, jnp.int32


def nt(a, b):
    return lax.dot_general(a, b, (((1,), (1,)), ((), ())), preferred_element_type=F32)


def nn(a, b):
    return jnp.dot(a, b, preferred_element_type=F32)


def iota(shape, dim):
    return lax.broadcasted_iota(I32, shape, dim)


def halves(x):
    hi = x.astype(BF16)
    return hi, (x - hi.astype(F32)).astype(BF16)


def hot(row, size):
    return (iota((size, row.shape[1]), 0) == row).astype(F32).astype(BF16)


def small_hot(row, size):
    which = iota((size, row.shape[1]), 0).astype(F32).astype(BF16)
    return jnp.where(which == row.astype(F32).astype(BF16), BF16(1), BF16(0))


def take(x, index):
    return jnp.take_along_axis(x, index, axis=1, mode="promise_in_bounds")


def tile_at(t, count=1):
    return pl.ds(pl.multiple_of(t * LANES, LANES), count * LANES)


def ranks(mask):
    tiles = mask.shape[0]
    upper_tri = (iota((LANES, LANES), 0) < iota((LANES, LANES), 1)).astype(F32).astype(BF16)
    lower_tri = (iota((tiles, tiles), 1) < iota((tiles, tiles), 0)).astype(F32).astype(BF16)
    half = mask.astype(BF16)
    before = jnp.sum(nn(lower_tri, half), axis=1, keepdims=True)
    return (nn(half, upper_tri) + before).astype(I32), before


def total_of(x):
    return jnp.sum(jnp.sum(x, axis=1, keepdims=True), axis=0, keepdims=True)


def react_kernel(
    states, mass, bins, cells, slots, rlist, rate_wt, stoich, scale_row, jac3,
    lower, upper, rank, base_v, solved,
    base_s, st, tail, index, low_rank, jac, rate_w, stoich_w, scale, packed, stack, sem, load_sems,
):
    species, count = states.shape
    tiles = count // LANES
    half = lower.shape[1]
    moved_tiles = 2 * half // LANES
    most = rlist.shape[1]
    groups = ROWS // 8
    part = count // LOADS
    loads = [
        pltpu.make_async_copy(
            states.at[:, pl.ds(i * part, part)], st.at[:, pl.ds(i * part, part)], load_sems.at[i]
        )
        for i in range(LOADS)
    ]
    for load in loads:
        load.start()

    r = rlist[...]
    listed = nt(hot(r >> 7, tiles), hot(r & 127, LANES))
    total = total_of(listed)
    moving = (slots[...] >= 0).astype(F32)
    total_move = total_of(moving)
    place, before = ranks(listed)
    place_move, before_move = ranks(moving)
    rank[...] = jnp.where(listed > 0, place, -1)
    lane = iota((tiles, LANES), 1)
    row = iota((tiles, LANES), 0)
    table = jnp.where(lane == 0, before, jnp.where(lane == 1, total, jnp.where(lane == 2, total_move, before_move)))
    for q in range(moved_tiles + 1):
        first = jnp.where((moving > 0) & (place_move == q * LANES), place.astype(F32) - total, 0.0)
        table = jnp.where((lane == 4) & (row == q), total_of(first) + total, table)
    base_v[...] = table.astype(I32)
    copy = pltpu.make_async_copy(base_v, base_s, sem)
    copy.start()
    low_rank[0] = jnp.where(listed > 0, place & 127, -1)
    low_rank[1] = jnp.where(moving > 0, place_move & 127, -1)

    scale[...] = jnp.transpose(jnp.broadcast_to(scale_row[...] * math.log(2.0), (LANES, scale_row.shape[1])))
    rate_w[...] = jnp.zeros_like(rate_w)
    rate_w[:, 0:species] = jnp.transpose(rate_wt[...].astype(F32)).astype(BF16)
    stoich_w[...] = jnp.zeros_like(stoich_w)
    stoich_w[0:species, :] = stoich[...]
    jac[...] = jnp.zeros_like(jac)
    for b in range(jac3.shape[1]):
        jac[0:species, b * ROWS : b * ROWS + species] = jac3[:, b, :]

    lanes8 = iota((8, LANES), 1).astype(F32).astype(BF16)

    def inverses(k, c):
        for u in range(UNROLL):
            t = k * UNROLL + u
            onehots = jnp.concatenate([small_hot(low_rank[s, pl.ds(t, 1), :], LANES) for s in range(2)], axis=0)
            at = pl.ds(pl.multiple_of(t * 8, 8), 8)
            index[at, :] = nt(lanes8, onehots).astype(I32)
        return c

    lax.fori_loop(0, tiles // UNROLL, inverses, 0)
    copy.wait()
    for load in loads:
        load.wait()
    rest = species - (groups - 1) * 8
    for t in range(tiles):
        at = slice(t * LANES, (t + 1) * LANES)
        rows = [mass[t : t + 1, :], (cells[t : t + 1, :] + 256 * bins[t : t + 1, :]).astype(F32),
                slots[t : t + 1, :].astype(F32), rank[t : t + 1, :].astype(F32)]
        tail[0:rest, at] = st[(groups - 1) * 8 : species, at]
        for i, value in enumerate(rows):
            tail[rest + i : rest + i + 1, at] = value

    lane8 = iota((8, LANES), 1)

    def source(g, t):
        if g == groups - 1:
            return tail[:, tile_at(t)]
        return st[8 * g : 8 * g + 8, tile_at(t)]

    def compact(out, column, which, total_at):
        def some(k, carry):
            for u in range(UNROLL):
                t = k * UNROLL + u
                first = base_s[t, column]
                after = jnp.where(t == tiles - 1, base_s[0, total_at], base_s[jnp.minimum(t + 1, tiles - 1), column])
                wraps = (after >> 7) != (first >> 7)
                inside = lane8 >= (first & 127)
                picks = index[pl.ds(pl.multiple_of(t * 8, 8), 8), which * LANES : (which + 1) * LANES]
                at = tile_at(first >> 7)
                fresh = []
                for g in range(groups):
                    got = take(source(g, t), picks)
                    new = jnp.where(inside, got, carry[g])
                    out[8 * g : 8 * g + 8, at] = new
                    fresh.append(jnp.where(wraps, got, new))
                carry = tuple(fresh)
            return carry

        carry = lax.fori_loop(
            0, tiles // UNROLL, some, tuple(jnp.zeros((8, LANES), F32) for _ in range(groups))
        )
        at = tile_at(base_s[0, total_at] >> 7)
        for g in range(groups):
            out[8 * g : 8 * g + 8, at] = carry[g]

    compact(solved, 0, 0, 1)
    compact(packed, 3, 1, 2)

    reactions = rate_w.shape[0]
    chunks = [(lo, min(CHUNK, reactions - lo)) for lo in range(0, reactions, CHUNK)]
    log2e = math.log2(math.e)

    def solve(k, c):
        subs = []
        for s in range(SUBS):
            at = pl.ds(pl.multiple_of((k * SUBS + s) * SUB, SUB), SUB)
            level = (solved[species + 1 : species + 2, at].astype(I32) >> 8).astype(F32)
            subs.append({"at": at, "start": solved[:, at], "level": level, "d": None})
        waiting = []

        def finish():
            sub, i, u = waiting.pop(0)
            lo, size = chunks[i]
            u = u * log2e
            soft = jnp.maximum(u, jnp.log2(1.0 + jnp.exp2(jnp.minimum(u, 126.0))))
            rate = (soft * scale[lo : lo + size, 0:1]).astype(BF16)
            term = nn(stoich_w[:, lo : lo + size], rate)
            sub["source"] = term if i == 0 else sub["source"] + term
            if i == len(chunks) - 1:
                d = sub["d"]
                residual = -CHEM_STEP * sub["source"]
                residual = (residual if d is None else d + residual).astype(BF16)
                masked = jnp.concatenate(
                    [jnp.where(sub["level"] == b, residual, BF16(0)) for b in range(jac3.shape[1])], axis=0
                )
                update = nn(jac[...], masked)
                sub["d"] = -update if d is None else d - update

        for sweep in range(NEWTON):
            for sub in subs:
                x = None
                for i, (lo, size) in enumerate(chunks):
                    if x is None:
                        x = (sub["start"] if sub["d"] is None else sub["start"] + sub["d"]).astype(BF16)
                    waiting.append((sub, i, nn(rate_w[lo : lo + size, :], x)))
                    if len(waiting) > LAG:
                        finish()
        while waiting:
            finish()
        for sub in subs:
            solved[:, sub["at"]] = sub["start"] + sub["d"]
        return c

    lax.fori_loop(0, (base_s[0, 1] + NCOL - 1) // NCOL, solve, 0)

    spans = []
    for q in range(moved_tiles):
        low, high = base_s[q, 4], base_s[q + 1, 4]
        spans.append((low >> 7, ((high - 1) >> 7) - (low >> 7) + 1))
    longest = functools.reduce(jnp.maximum, [s[1] for s in spans])
    final = most // LANES - 1

    def expand(s, c):
        for q in range(moved_tiles):
            here = slice(q * LANES, (q + 1) * LANES)
            t = jnp.minimum(spans[q][0] + s, final)
            wanted = packed[ROWS - 1 : ROWS, here].astype(I32)
            wanted = jnp.broadcast_to(jnp.where(lane8[0:1] + q * LANES < base_s[0, 2], wanted, -1), (8, LANES))
            mine = (wanted >> 7) == t
            picks = wanted & 127
            for g in range(groups):
                rows = slice(8 * g, 8 * g + 8)
                keep = mine if g < groups - 1 else mine & (iota((8, LANES), 0) < rest)
                packed[rows, here] = jnp.where(keep, take(solved[rows, tile_at(t)], picks), packed[rows, here])
        return c

    lax.fori_loop(0, longest, expand, 0)

    mine = packed[:, 0 : 2 * half]
    filled = iota((1, 2 * half), 1) < base_s[0, 2]
    mine = jnp.where(filled, mine, 0.0)
    hi, lo = halves(mine)
    stack[0:ROWS, :] = hi
    stack[ROWS:, :] = lo
    slot = jnp.where(filled, mine[species + 2 : species + 3].astype(I32), -1)
    for out, first in ((lower, 0), (upper, half)):
        moved = nt(stack[...], hot_rows(slot - first, half))
        out[...] = moved[0:ROWS] + moved[ROWS:]


def hot_rows(row, size):
    return (iota((size, row.shape[1]), 0) == row).astype(F32).astype(BF16)


def cell_sums(x, w, cell, n_cells):
    hi, lo = halves(x * w)
    onehot = small_hot(cell, n_cells)
    return nt(jnp.concatenate([hi, lo], axis=0), onehot)


def with_ones(x):
    width = x.shape[1]
    return jnp.concatenate([x, jnp.ones((1, width), F32), jnp.zeros((ROWS - x.shape[0] - 1, width), F32)], axis=0)


def sums_kernel(base, states, rank, solved, mass, cells, slots, reacted, sums):
    species, width = states.shape
    groups = ROWS // 8
    step = pl.program_id(0)
    lane8 = iota((8, LANES), 1)

    for b in range(width // LANES):
        here = slice(b * LANES, (b + 1) * LANES)
        first = base[step * (width // LANES) + b, 0]
        t = first >> 7
        inside = lane8 >= (first & 127)
        wanted = jnp.broadcast_to(rank[b : b + 1, :], (8, LANES))
        picks = wanted & 127
        mine = wanted >= 0
        for g in range(groups):
            n = min(8, species - 8 * g)
            rows = slice(8 * g, 8 * g + n)
            pair = jnp.where(inside[:n], solved[rows, tile_at(t)], solved[rows, tile_at(t + 1)])
            reacted[rows, here] = jnp.where(mine[:n], take(pair, picks[:n]), states[rows, here])
    w = jnp.where(slots[...] < 0, mass[...], 0.0)
    term = cell_sums(with_ones(reacted[...]), w, cells[...], sums.shape[1])

    @pl.when(step == 0)
    def _():
        sums[...] = term

    @pl.when(step > 0)
    def _():
        sums[...] += term


def arrival(ref, species):
    w = ref[species : species + 1, :]
    cell = ref[species + 1 : species + 2, :].astype(I32) & 255
    return ref[0:species, :], w, jnp.where(w > 0, cell, -1)


def mix_kernel(reacted, cells, slots, below, above, sums, mixing, mixed, means, table):
    species = reacted.shape[0]
    n_cells = sums.shape[1]
    step = pl.program_id(0)
    last = pl.num_programs(0) - 1

    @pl.when(step == 0)
    def _():
        acc = sums[...]
        for ref in (below, above):
            x, w, cell = arrival(ref, species)
            acc = acc + cell_sums(with_ones(x), w, cell, n_cells)
        acc = acc[0:ROWS] + acc[ROWS:]
        mean = acc[0:species] / acc[species : species + 1]
        means[...] = mean
        keep = jnp.exp(-MIX_RATE * mixing[...])
        table[...] = jnp.zeros_like(table)
        hi, lo = halves(mean * (1.0 - keep))
        table[0:species, 0:n_cells] = hi
        table[0:species, n_cells:] = lo
        hi, lo = halves(jnp.broadcast_to(keep, (16, n_cells)))
        table[ROWS:, 0:n_cells] = hi
        table[ROWS:, n_cells:] = lo

    def blend(x, cell):
        onehot = small_hot(cell, n_cells)
        pulled = nn(table[...], jnp.concatenate([onehot, onehot], axis=0))
        return x * pulled[ROWS : ROWS + 1] + pulled[:species]

    @pl.when(step < last)
    def _():
        mixed[...] = blend(reacted[...], jnp.where(slots[...] < 0, cells[...], -1))

    @pl.when(step == last)
    def _():
        half = below.shape[1]
        for ref, at in ((below, slice(0, half)), (above, slice(half, 2 * half))):
            x, _, cell = arrival(ref, species)
            mixed[:, at] = blend(x, cell)


def body(
    states, particle_mass, bin_index, cell_index, move_slot, react_list,
    rate_weights, stoichiometry, rate_scale, jacobian_inverse, mixing_rate, slot_count,
):
    species, count = states.shape
    n_cells = mixing_rate.shape[0]
    listed = react_list.shape[0]
    reactions = rate_scale.shape[0]
    n_bins = jacobian_inverse.shape[0]
    tiles = count // LANES
    wide = listed + 2 * LANES
    half = slot_count // 2
    square = lambda a: a.reshape(tiles, LANES)
    line = lambda a: a.reshape(1, -1)
    vmem = pl.BlockSpec(memory_space=pltpu.VMEM)
    lower, upper, rank, base, solved = pl.pallas_call(
        react_kernel,
        in_specs=[pl.BlockSpec(memory_space=pl.ANY)] + [vmem] * 9,
        out_shape=(
            jax.ShapeDtypeStruct((ROWS, half), F32),
            jax.ShapeDtypeStruct((ROWS, half), F32),
            jax.ShapeDtypeStruct((tiles, LANES), I32),
            jax.ShapeDtypeStruct((tiles, LANES), I32),
            jax.ShapeDtypeStruct((ROWS, wide), F32),
        ),
        scratch_shapes=[
            pltpu.SMEM((tiles, LANES), I32),
            pltpu.VMEM((species, count), F32),
            pltpu.VMEM((8, count), F32),
            pltpu.VMEM((tiles * 8, 2 * LANES), I32),
            pltpu.VMEM((2, tiles, LANES), I32),
            pltpu.VMEM((ROWS, n_bins * ROWS), BF16),
            pltpu.VMEM((reactions, ROWS), BF16),
            pltpu.VMEM((ROWS, reactions), BF16),
            pltpu.VMEM((reactions, LANES), F32),
            pltpu.VMEM((ROWS, slot_count + 2 * LANES), F32),
            pltpu.VMEM((2 * ROWS, slot_count), BF16),
            pltpu.SemaphoreType.DMA,
            pltpu.SemaphoreType.DMA((LOADS,)),
        ],
        compiler_params=pltpu.CompilerParams(vmem_limit_bytes=40 * 2**20),
        name="react",
    )(
        states, square(particle_mass), square(bin_index), square(cell_index), square(move_slot),
        line(react_list), rate_weights.T, stoichiometry, line(rate_scale), jnp.transpose(jacobian_inverse, (1, 0, 2)),
    )
    devices = lax.axis_size("dev")
    below = lax.ppermute(upper, "dev", [(i, i + 1) for i in range(devices - 1)])
    above = lax.ppermute(lower, "dev", [(i + 1, i) for i in range(devices - 1)])
    width = slot_count
    steps = count // width
    own = lambda rows: pl.BlockSpec((rows, width), lambda i: (0, jnp.minimum(i, steps - 1)))
    whole = lambda shape: pl.BlockSpec(shape, lambda i: (0, 0))
    masses, cell_line, slot_line = line(particle_mass), line(cell_index), line(move_slot)
    reacted, sums = pl.pallas_call(
        sums_kernel,
        grid=(steps,),
        in_specs=[
            pl.BlockSpec(memory_space=pltpu.SMEM), own(species),
            pl.BlockSpec((width // LANES, LANES), lambda i: (i, 0)),
            whole((ROWS, wide)), own(1), own(1), own(1),
        ],
        out_specs=(own(species), whole((2 * ROWS, n_cells))),
        out_shape=(jax.ShapeDtypeStruct((species, count), F32), jax.ShapeDtypeStruct((2 * ROWS, n_cells), F32)),
        compiler_params=pltpu.CompilerParams(vmem_limit_bytes=32 * 2**20),
        cost_estimate=pl.CostEstimate(
            flops=4 * ROWS * count * n_cells, bytes_accessed=8 * species * count, transcendentals=0
        ),
        name="sums",
    )(base, states, rank, solved, masses, cell_line, slot_line)
    mixed, means = pl.pallas_call(
        mix_kernel,
        grid=(steps + 1,),
        in_specs=[
            own(species), own(1), own(1),
            whole((ROWS, half)), whole((ROWS, half)), whole((2 * ROWS, n_cells)), whole((1, n_cells)),
        ],
        out_specs=(pl.BlockSpec((species, width), lambda i: (0, i)), whole((species, n_cells))),
        out_shape=(
            jax.ShapeDtypeStruct((species, count + slot_count), F32),
            jax.ShapeDtypeStruct((species, n_cells), F32),
        ),
        scratch_shapes=[pltpu.VMEM((ROWS + 16, 2 * n_cells), BF16)],
        compiler_params=pltpu.CompilerParams(vmem_limit_bytes=32 * 2**20),
        name="mix",
    )(reacted, cell_line, slot_line, below, above, sums, line(mixing_rate))
    return mixed, means


MCAP = 512


def solution(mesh):
    each, all_of = P("dev"), P()
    return jax.shard_map(
        functools.partial(body, slot_count=2 * MCAP),
        mesh=mesh,
        in_specs=(P(None, "dev"), each, each, each, each, each, all_of, all_of, all_of, all_of, each),
        out_specs=(P(None, "dev"), P(None, "dev")),
        check_vma=False,
    )
```

profile of v0, /device:TPU:1, one launch (start us, length us, event | category | flops | bytes accessed | tf_op | source)
XLA Modules:
  0.0 57.1 jit_solution(6673532628965927974)
XLA Ops:
  0.6 0.0 copy-start
  0.6 2.8 %copy-done = f32[188,8192]{1,0:T(8,128)S(1)} copy-done((f32[188,8192]{1,0:T(8,128)S(1)}, f32[188,8192]{1,0:T(8,128)}, u32[]{:S(2)}) %copy-start) | copy-done | bytes 6160408
  3.4 0.0 copy-start.2
  3.4 1.0 %copy-done.2 = bf16[939,188]{0,1:T(8,128)(2,1)S(1)} copy-done((bf16[939,188]{0,1:T(8,128)(2,1)S(1)}, bf16[939,188]{0,1:T(8,128)(2,1)}, u32[]{:S(2)}) %copy-start.2) | copy-done | bytes 353088
  4.4 0.0 copy-start.3
  4.4 1.0 %copy-done.3 = bf16[188,939]{1,0:T(8,128)(2,1)S(1)} copy-done((bf16[188,939]{1,0:T(8,128)(2,1)S(1)}, bf16[188,939]{1,0:T(8,128)(2,1)}, u32[]{:S(2)}) %copy-start.3) | copy-done | bytes 353088
  5.4 0.0 copy-start.4
  5.4 1.0 %copy-done.4 = bf16[4,188,188]{2,0,1:T(4,128)(2,1)S(1)} copy-done((bf16[4,188,188]{2,0,1:T(4,128)(2,1)S(1)}, bf16[4,188,188]{2,0,1:T(4,128)(2,1)}, u32[]{:S(2)}) %copy-start.4) | copy-done | bytes 282776
  6.4 0.0 copy-start.5
  6.4 0.8 %copy-done.5 = s32[8192]{0:T(1024)S(1)} copy-done((s32[8192]{0:T(1024)S(1)}, s32[8192]{0:T(1024)}, u32[]{:S(2)}) %copy-start.5) | copy-done | bytes 32792
  7.2 0.0 copy-start.6
  7.2 0.8 %copy-done.6 = s32[8192]{0:T(1024)S(1)} copy-done((s32[8192]{0:T(1024)S(1)}, s32[8192]{0:T(1024)}, u32[]{:S(2)}) %copy-start.6) | copy-done | bytes 32792
  7.9 0.0 copy-start.7
  7.9 0.8 %copy-done.7 = f32[8192]{0:T(1024)S(1)} copy-done((f32[8192]{0:T(1024)S(1)}, f32[8192]{0:T(1024)}, u32[]{:S(2)}) %copy-start.7) | copy-done | bytes 32792
  8.7 0.0 copy-start.8
  8.7 0.8 %copy-done.8 = s32[8192]{0:T(1024)S(1)} copy-done((s32[8192]{0:T(1024)S(1)}, s32[8192]{0:T(1024)}, u32[]{:S(2)}) %copy-start.8) | copy-done | bytes 32792
  9.4 0.0 copy-start.9
  9.4 0.7 %copy-done.9 = s32[2048]{0:T(1024)S(1)} copy-done((s32[2048]{0:T(1024)S(1)}, s32[2048]{0:T(1024)}, u32[]{:S(2)}) %copy-start.9) | copy-done | bytes 8216
  10.1 0.0 copy-start.10
  10.1 0.7 %copy-done.10 = f32[939]{0:T(1024)S(1)} copy-done((f32[939]{0:T(1024)S(1)}, f32[939]{0:T(1024)}, u32[]{:S(2)}) %copy-start.10) | copy-done | bytes 3780
  10.8 0.0 copy-start.1
  10.8 0.0 copy-start.11
  10.8 16.6 %react.1 = (f32[192,512]{1,0:T(8,128)S(1)}, f32[192,512]{1,0:T(8,128)S(1)}, s32[64,128]{1,0:T(8,128)S(1)}, s32[64,128]{1,0:T(8,128)S(1)}, f32[192,2304]{1,0:T(8,128)S(1)}) custom-call(f32[188,8192]{1,0:T(8,128)S(1)} %copy-done, f32[64,128]{1,0:T(8,128)S(1)} %bitcast.20, s32[64,128]{1,0:T(8,128)S(1)} %bitcast.22, s32[64,128]{1,0:T(8,128)S(1)} %bitcast.14, ...), custom_call_target="tpu_custom_call" | custom-call | tf_op jit(solution)/shard_map/react/pallas_call | solution.py:371
  27.4 11.3 %collective-permute-start = (f32[192,512]{1,0:T(8,128)S(1)}, f32[192,512]{1,0:T(8,128)S(1)}, u32[]{:S(2)}, u32[]{:S(2)}) collective-permute-start(f32[192,512]{1,0:T(8,128)S(1)} %get-tuple-element.13), channel_id=1, source_target_pairs={{0,1},{1,2},{2,3},{3,4},{4,5},{5,6},{6,7},{7,8},{8,9},{9,10},{10,1... | collective-permute-start | bytes 1179656 | tf_op jit(solution)/shard_map/ppermute | solution.py:403
  38.8 1.9 %collective-permute-start.1 = (f32[192,512]{1,0:T(8,128)S(1)}, f32[192,512]{1,0:T(8,128)S(1)}, u32[]{:S(2)}, u32[]{:S(2)}) collective-permute-start(f32[192,512]{1,0:T(8,128)S(1)} %get-tuple-element.14), channel_id=1, source_target_pairs={{1,0},{2,1},{3,2},{4,3},{5,4},{6,5},{7,6},{8,7},{9,8},{10,9},{11,1... | collective-permute-start | bytes 1179656 | tf_op jit(solution)/shard_map/ppermute | solution.py:404
  40.7 0.0 copy-done.1
  40.7 8.2 %sums.1 = (f32[188,8192]{1,0:T(8,128)S(1)}, f32[384,256]{1,0:T(8,128)S(1)}) custom-call(s32[64,128]{1,0:T(8,128)S(1)} %get-tuple-element.9.base, f32[188,8192]{1,0:T(8,128)S(1)} %copy-done.1, s32[64,128]{1,0:T(8,128)S(1)} %get-tuple-element.10.rank, f32[192,2304]{1,0:T(8,128)S(1)} %get-tuple-element.11.solved, f32[1,8192]{1,0:T(1,128)S(1)} %bitcast.21, ...), custom_call_target="tpu_custom_call" | custom-call | flops 1610612736 | bytes 12320768 | tf_op jit(solution)/shard_map/sums/pallas_call | solution.py:410
  48.9 0.0 collective-permute-done.below
  48.9 0.7 %collective-permute-done.1.above = f32[192,512]{1,0:T(8,128)S(1)} collective-permute-done((f32[192,512]{1,0:T(8,128)S(1)}, f32[192,512]{1,0:T(8,128)S(1)}, u32[]{:S(2)}, u32[]{:S(2)}) %collective-permute-start.1) | collective-permute-done | bytes 393248 | tf_op jit(solution)/shard_map/ppermute | solution.py:404
  49.6 0.0 copy-done.11
  49.6 7.5 %mix.1 = (f32[188,9216]{1,0:T(8,128)}, f32[188,256]{1,0:T(8,128)}) custom-call(f32[188,8192]{1,0:T(8,128)S(1)} %get-tuple-element.12.reacted, s32[1,8192]{1,0:T(1,128)S(1)} %bitcast.16, s32[1,8192]{1,0:T(1,128)S(1)} %bitcast.19, f32[192,512]{1,0:T(8,128)S(1)} %collective-permute-done.below, f32[192,512]{1,0:T(8,128)S(1)} %collective-permute-done.1.above, ...), custom_call_target="tpu_custom_call" | custom-call | tf_op jit(solution)/shard_map/mix/pallas_call | solution.py:426
Async XLA Ops:
  0.6 2.8 %copy-start = (f32[188,8192]{1,0:T(8,128)S(1)}, f32[188,8192]{1,0:T(8,128)}, u32[]{:S(2)}) copy-start(f32[188,8192]{1,0:T(8,128)} %states.3) | copy-start | bytes 18481156
  3.4 1.0 %copy-start.2 = (bf16[939,188]{0,1:T(8,128)(2,1)S(1)}, bf16[939,188]{0,1:T(8,128)(2,1)}, u32[]{:S(2)}) copy-start(bf16[939,188]{0,1:T(8,128)(2,1)} %param.17) | copy-start | bytes 1059196
  4.4 1.0 %copy-start.3 = (bf16[188,939]{1,0:T(8,128)(2,1)S(1)}, bf16[188,939]{1,0:T(8,128)(2,1)}, u32[]{:S(2)}) copy-start(bf16[188,939]{1,0:T(8,128)(2,1)} %stoich.1) | copy-start | bytes 1059196
  5.4 1.0 %copy-start.4 = (bf16[4,188,188]{2,0,1:T(4,128)(2,1)S(1)}, bf16[4,188,188]{2,0,1:T(4,128)(2,1)}, u32[]{:S(2)}) copy-start(bf16[4,188,188]{2,0,1:T(4,128)(2,1)} %param.20) | copy-start | bytes 848260
  6.4 0.8 %copy-start.5 = (s32[8192]{0:T(1024)S(1)}, s32[8192]{0:T(1024)}, u32[]{:S(2)}) copy-start(s32[8192]{0:T(1024)} %param.14) | copy-start | bytes 98308
  7.2 0.8 %copy-start.6 = (s32[8192]{0:T(1024)S(1)}, s32[8192]{0:T(1024)}, u32[]{:S(2)}) copy-start(s32[8192]{0:T(1024)} %param.15) | copy-start | bytes 98308
  7.9 0.8 %copy-start.7 = (f32[8192]{0:T(1024)S(1)}, f32[8192]{0:T(1024)}, u32[]{:S(2)}) copy-start(f32[8192]{0:T(1024)} %param.12) | copy-start | bytes 98308
  8.7 0.8 %copy-start.8 = (s32[8192]{0:T(1024)S(1)}, s32[8192]{0:T(1024)}, u32[]{:S(2)}) copy-start(s32[8192]{0:T(1024)} %param.13) | copy-start | bytes 98308
  9.4 0.7 %copy-start.9 = (s32[2048]{0:T(1024)S(1)}, s32[2048]{0:T(1024)}, u32[]{:S(2)}) copy-start(s32[2048]{0:T(1024)} %param.16) | copy-start | bytes 24580
  10.1 0.7 %copy-start.10 = (f32[939]{0:T(1024)S(1)}, f32[939]{0:T(1024)}, u32[]{:S(2)}) copy-start(f32[939]{0:T(1024)} %param.19) | copy-start | bytes 11272
  10.8 29.9 %copy-start.1 = (f32[188,8192]{1,0:T(8,128)S(1)}, f32[188,8192]{1,0:T(8,128)}, u32[]{:S(2)}) copy-start(f32[188,8192]{1,0:T(8,128)} %states.3) | copy-start | bytes 18481156
  10.8 38.8 %copy-start.11 = (f32[256]{0:T(256)S(1)}, f32[256]{0:T(256)}, u32[]{:S(2)}) copy-start(f32[256]{0:T(256)} %param.21) | copy-start | bytes 3076
  27.4 21.5 %collective-permute-start = (f32[192,512]{1,0:T(8,128)S(1)}, f32[192,512]{1,0:T(8,128)S(1)}, u32[]{:S(2)}, u32[]{:S(2)}) collective-permute-start(f32[192,512]{1,0:T(8,128)S(1)} %get-tuple-element.13), channel_id=1, source_target_pairs={{0,1},{1,2},{2,3},{3,4},{4,5},{5,6},{6,7},{7,8},{8,9},{9,10},{10,1... | collective-permute-start | bytes 1179656 | tf_op jit(solution)/shard_map/ppermute | solution.py:403
  38.8 10.8 %collective-permute-start.1 = (f32[192,512]{1,0:T(8,128)S(1)}, f32[192,512]{1,0:T(8,128)S(1)}, u32[]{:S(2)}, u32[]{:S(2)}) collective-permute-start(f32[192,512]{1,0:T(8,128)S(1)} %get-tuple-element.14), channel_id=1, source_target_pairs={{1,0},{2,1},{3,2},{4,3},{5,4},{6,5},{7,6},{8,7},{9,8},{10,9},{11,1... | collective-permute-start | bytes 1179656 | tf_op jit(solution)/shard_map/ppermute | solution.py:404
where the time goes:
time: 57.9 us; the launch traced here: 57.1 us
  Pallas kernels  32.3 us (56%)
  starting transfers between devices  13.3 us (23%)
  local copies, waits for them, and re-layouts  10.2 us (18%)
  between operations  0.7 us (1%)
  waiting for transfers between devices  0.67 us (1%)
    pallas_call x1, Pallas kernels, body(): pl.pallas_call(react_kernel, in_specs=[pl.BlockSpec(memory_space=pl.ANY)]...  16.6 us
    ppermute x1, starting transfers between devices, body(): below = lax.ppermute(upper, 'dev', [(i, i + 1) for i in range(devices - 1)])  11.3 us
    unnamed x24, local copies, waits for them, and re-layouts  10.2 us
    pallas_call x1, Pallas kernels, body(): pl.pallas_call(sums_kernel, grid=(steps,), in_specs=[pl.BlockSpec(memory_...  8.2 us
    pallas_call x1, Pallas kernels, body(): pl.pallas_call(mix_kernel, grid=(steps + 1,), in_specs=[own(species), own...  7.52 us
    ppermute x1, starting transfers between devices, body(): above = lax.ppermute(lower, 'dev', [(i + 1, i) for i in range(devices - 1)])  1.92 us
  transfers between devices with their start and end apart: 2, of which 1 were waited for; matrix products, arithmetic and copies ran while one was open for 0% of the time, Pallas kernels for 14%

commit v1 on v0

--- a/solution.py
+++ b/solution.py
@@ -19,6 +19,8 @@
 ROWS = 192
 UNROLL = 8
 LOADS = 4
+SMALL = 9
+EARLY = 2
 F32, BF16, I32 = jnp.float32, jnp.bfloat16, jnp.int32
 
 
@@ -70,10 +72,13 @@
 
 
 def react_kernel(
-    states, mass, bins, cells, slots, rlist, rate_wt, stoich, scale_row, jac3,
-    lower, upper, rank, base_v, solved,
-    base_s, st, tail, index, low_rank, jac, rate_w, stoich_w, scale, packed, stack, sem, load_sems,
+    states, *refs,
 ):
+    small, refs = refs[:SMALL], refs[SMALL:]
+    lower, upper, base_v, solved, *refs = refs
+    held, refs = refs[:SMALL], refs[SMALL:]
+    slots, rlist, mass, bins, cells, scale_row, rate_wt, stoich, jac3 = held
+    (base_s, st, rank, tail, index, low_rank, jac, rate_w, stoich_w, scale, packed, stack, sem, load_sems, small_sems) = refs
     species, count = states.shape
     tiles = count // LANES
     half = lower.shape[1]
@@ -87,8 +92,11 @@
         )
         for i in range(LOADS)
     ]
-    for load in loads:
-        load.start()
+    fetches = [pltpu.make_async_copy(small[i], held[i], small_sems.at[i]) for i in range(SMALL)]
+    for copy in fetches[:EARLY] + loads + fetches[EARLY:]:
+        copy.start()
+    for copy in fetches[:EARLY]:
+        copy.wait()
 
     r = rlist[...]
     listed = nt(hot(r >> 7, tiles), hot(r & 127, LANES))
@@ -105,12 +113,14 @@
         first = jnp.where((moving > 0) & (place_move == q * LANES), place.astype(F32) - total, 0.0)
         table = jnp.where((lane == 4) & (row == q), total_of(first) + total, table)
     base_v[...] = table.astype(I32)
-    copy = pltpu.make_async_copy(base_v, base_s, sem)
-    copy.start()
+    bases = pltpu.make_async_copy(base_v, base_s, sem)
+    bases.start()
     low_rank[0] = jnp.where(listed > 0, place & 127, -1)
     low_rank[1] = jnp.where(moving > 0, place_move & 127, -1)
 
-    scale[...] = jnp.transpose(jnp.broadcast_to(scale_row[...] * math.log(2.0), (LANES, scale_row.shape[1])))
+    for copy in fetches[EARLY:]:
+        copy.wait()
+    scale[...] = jnp.transpose(jnp.broadcast_to(scale_row[...], (LANES, scale_row.shape[1])))
     rate_w[...] = jnp.zeros_like(rate_w)
     rate_w[:, 0:species] = jnp.transpose(rate_wt[...].astype(F32)).astype(BF16)
     stoich_w[...] = jnp.zeros_like(stoich_w)
@@ -130,7 +140,7 @@
         return c
 
     lax.fori_loop(0, tiles // UNROLL, inverses, 0)
-    copy.wait()
+    bases.wait()
     for load in loads:
         load.wait()
     rest = species - (groups - 1) * 8
@@ -138,6 +148,8 @@
         at = slice(t * LANES, (t + 1) * LANES)
         rows = [mass[t : t + 1, :], (cells[t : t + 1, :] + 256 * bins[t : t + 1, :]).astype(F32),
                 slots[t : t + 1, :].astype(F32), rank[t : t + 1, :].astype(F32)]
+        per = tiles // 8
+        solved[ROWS + t // per : ROWS + t // per + 1, t % per * LANES : (t % per + 1) * LANES] = rows[3]
         tail[0:rest, at] = st[(groups - 1) * 8 : species, at]
         for i, value in enumerate(rows):
             tail[rest + i : rest + i + 1, at] = value
@@ -180,21 +192,19 @@
 
     reactions = rate_w.shape[0]
     chunks = [(lo, min(CHUNK, reactions - lo)) for lo in range(0, reactions, CHUNK)]
-    log2e = math.log2(math.e)
 
     def solve(k, c):
         subs = []
         for s in range(SUBS):
             at = pl.ds(pl.multiple_of((k * SUBS + s) * SUB, SUB), SUB)
             level = (solved[species + 1 : species + 2, at].astype(I32) >> 8).astype(F32)
-            subs.append({"at": at, "start": solved[:, at], "level": level, "d": None})
+            subs.append({"at": at, "start": solved[0:ROWS, at], "level": level, "d": None})
         waiting = []
 
         def finish():
             sub, i, u = waiting.pop(0)
             lo, size = chunks[i]
-            u = u * log2e
-            soft = jnp.maximum(u, jnp.log2(1.0 + jnp.exp2(jnp.minimum(u, 126.0))))
+            soft = jnp.maximum(u, jnp.log(1.0 + jnp.exp(jnp.minimum(u, 87.0))))
             rate = (soft * scale[lo : lo + size, 0:1]).astype(BF16)
             term = nn(stoich_w[:, lo : lo + size], rate)
             sub["source"] = term if i == 0 else sub["source"] + term
@@ -220,7 +230,7 @@
         while waiting:
             finish()
         for sub in subs:
-            solved[:, sub["at"]] = sub["start"] + sub["d"]
+            solved[0:ROWS, sub["at"]] = sub["start"] + sub["d"]
         return c
 
     lax.fori_loop(0, (base_s[0, 1] + NCOL - 1) // NCOL, solve, 0)
@@ -275,7 +285,7 @@
     return jnp.concatenate([x, jnp.ones((1, width), F32), jnp.zeros((ROWS - x.shape[0] - 1, width), F32)], axis=0)
 
 
-def sums_kernel(base, states, rank, solved, mass, cells, slots, reacted, sums):
+def sums_kernel(base, states, solved, mass, cells, slots, reacted, sums):
     species, width = states.shape
     groups = ROWS // 8
     step = pl.program_id(0)
@@ -286,7 +296,8 @@
         first = base[step * (width // LANES) + b, 0]
         t = first >> 7
         inside = lane8 >= (first & 127)
-        wanted = jnp.broadcast_to(rank[b : b + 1, :], (8, LANES))
+        wanted = jnp.where(iota((8, LANES), 0) == step, solved[ROWS : ROWS + 8, here], 0.0)
+        wanted = jnp.broadcast_to(jnp.sum(wanted, axis=0, keepdims=True), (8, LANES)).astype(I32)
         picks = wanted & 127
         mine = wanted >= 0
         for g in range(groups):
@@ -367,20 +378,23 @@
     half = slot_count // 2
     square = lambda a: a.reshape(tiles, LANES)
     line = lambda a: a.reshape(1, -1)
-    vmem = pl.BlockSpec(memory_space=pltpu.VMEM)
-    lower, upper, rank, base, solved = pl.pallas_call(
+    small = [
+        square(move_slot), line(react_list), square(particle_mass), square(bin_index), square(cell_index),
+        line(rate_scale), rate_weights.T, stoichiometry, jnp.transpose(jacobian_inverse, (1, 0, 2)),
+    ]
+    lower, upper, base, solved = pl.pallas_call(
         react_kernel,
-        in_specs=[pl.BlockSpec(memory_space=pl.ANY)] + [vmem] * 9,
+        in_specs=[pl.BlockSpec(memory_space=pltpu.HBM)] * (1 + SMALL),
         out_shape=(
             jax.ShapeDtypeStruct((ROWS, half), F32),
             jax.ShapeDtypeStruct((ROWS, half), F32),
             jax.ShapeDtypeStruct((tiles, LANES), I32),
-            jax.ShapeDtypeStruct((tiles, LANES), I32),
-            jax.ShapeDtypeStruct((ROWS, wide), F32),
+            jax.ShapeDtypeStruct((ROWS + 8, wide), F32),
         ),
-        scratch_shapes=[
+        scratch_shapes=[pltpu.VMEM(a.shape, a.dtype) for a in small] + [
             pltpu.SMEM((tiles, LANES), I32),
             pltpu.VMEM((species, count), F32),
+            pltpu.VMEM((tiles, LANES), I32),
             pltpu.VMEM((8, count), F32),
             pltpu.VMEM((tiles * 8, 2 * LANES), I32),
             pltpu.VMEM((2, tiles, LANES), I32),
@@ -392,13 +406,11 @@
             pltpu.VMEM((2 * ROWS, slot_count), BF16),
             pltpu.SemaphoreType.DMA,
             pltpu.SemaphoreType.DMA((LOADS,)),
+            pltpu.SemaphoreType.DMA((SMALL,)),
         ],
-        compiler_params=pltpu.CompilerParams(vmem_limit_bytes=40 * 2**20),
+        compiler_params=pltpu.CompilerParams(vmem_limit_bytes=54 * 2**20),
         name="react",
-    )(
-        states, square(particle_mass), square(bin_index), square(cell_index), square(move_slot),
-        line(react_list), rate_weights.T, stoichiometry, line(rate_scale), jnp.transpose(jacobian_inverse, (1, 0, 2)),
-    )
+    )(states, *small)
     devices = lax.axis_size("dev")
     below = lax.ppermute(upper, "dev", [(i, i + 1) for i in range(devices - 1)])
     above = lax.ppermute(lower, "dev", [(i + 1, i) for i in range(devices - 1)])
@@ -411,9 +423,7 @@
         sums_kernel,
         grid=(steps,),
         in_specs=[
-            pl.BlockSpec(memory_space=pltpu.SMEM), own(species),
-            pl.BlockSpec((width // LANES, LANES), lambda i: (i, 0)),
-            whole((ROWS, wide)), own(1), own(1), own(1),
+            pl.BlockSpec(memory_space=pltpu.SMEM), own(species), whole((ROWS + 8, wide)), own(1), own(1), own(1),
         ],
         out_specs=(own(species), whole((2 * ROWS, n_cells))),
         out_shape=(jax.ShapeDtypeStruct((species, count), F32), jax.ShapeDtypeStruct((2 * ROWS, n_cells), F32)),
@@ -422,7 +432,7 @@
             flops=4 * ROWS * count * n_cells, bytes_accessed=8 * species * count, transcendentals=0
         ),
         name="sums",
-    )(base, states, rank, solved, masses, cell_line, slot_line)
+    )(base, states, solved, masses, cell_line, slot_line)
     mixed, means = pl.pallas_call(
         mix_kernel,
         grid=(steps + 1,),

time: 57.9 us -> 53.2 us (0.919)
  the two profiles are of different devices: /device:TPU:1 before, /device:TPU:16 now
where the time goes in v1:
time: 53.2 us; the launch traced here: 53 us
  Pallas kernels  42.5 us (80%)
  starting transfers between devices  7.36 us (14%)
  local copies, waits for them, and re-layouts  2.28 us (4%)
  between operations  0.77 us (1%)
    pallas_call x1, Pallas kernels, body(): pl.pallas_call(react_kernel, in_specs=[pl.BlockSpec(memory_space=pltpu.HB...  26.7 us
    pallas_call x1, Pallas kernels, body(): pl.pallas_call(sums_kernel, grid=(steps,), in_specs=[pl.BlockSpec(memory_...  8.26 us
    pallas_call x1, Pallas kernels, body(): pl.pallas_call(mix_kernel, grid=(steps + 1,), in_specs=[own(species), own...  7.54 us
    ppermute x1, starting transfers between devices, body(): above = lax.ppermute(lower, 'dev', [(i + 1, i) for i in range(devices - 1)])  5.44 us
    unnamed x14, local copies, waits for them, and re-layouts  2.28 us
    ppermute x1, starting transfers between devices, body(): below = lax.ppermute(upper, 'dev', [(i, i + 1) for i in range(devices - 1)])  1.92 us
  transfers between devices with their start and end apart: 2, of which 0 were waited for; matrix products, arithmetic and copies ran while one was open for 0% of the time, Pallas kernels for 16%

profile of v1, /device:TPU:16, one launch (start us, length us, event | category | flops | bytes accessed | tf_op | source)
XLA Modules:
  0.0 53.0 jit_solution(17888561263772540106)
XLA Ops:
  0.6 0.0 copy-start
  0.6 0.0 copy-start.4
  0.7 0.0 copy-start.3
  0.7 0.0 copy-start.2
  0.7 0.0 copy-start.6
  0.7 26.7 %react.1 = (f32[192,512]{1,0:T(8,128)}, f32[192,512]{1,0:T(8,128)}, s32[64,128]{1,0:T(8,128)}, f32[200,2304]{1,0:T(8,128)}) custom-call(f32[188,8192]{1,0:T(8,128)} %states.3, s32[64,128]{1,0:T(8,128)} %bitcast.12, s32[1,2048]{1,0:T(1,128)} %bitcast.24, f32[64,128]{1,0:T(8,128)} %bitcast.18, s32[64,128]{1,0:T(8,128)} %bitcast.23, s32[64,128]{1,0:T(8,128)} %bitcast.15, ...), custom_call_target="tpu_custom_call" | custom-call | tf_op jit(solution)/shard_map/react/pallas_call | solution.py:385
  27.4 1.9 %collective-permute-start = (f32[192,512]{1,0:T(8,128)}, f32[192,512]{1,0:T(8,128)S(1)}, u32[]{:S(2)}, u32[]{:S(2)}) collective-permute-start(f32[192,512]{1,0:T(8,128)} %get-tuple-element.11), channel_id=1, source_target_pairs={{0,1},{1,2},{2,3},{3,4},{4,5},{5,6},{6,7},{7,8},{8,9},{9,10},{10,1... | collective-permute-start | bytes 1179656 | tf_op jit(solution)/shard_map/ppermute | solution.py:415
  29.4 5.4 %collective-permute-start.1 = (f32[192,512]{1,0:T(8,128)}, f32[192,512]{1,0:T(8,128)S(1)}, u32[]{:S(2)}, u32[]{:S(2)}) collective-permute-start(f32[192,512]{1,0:T(8,128)} %get-tuple-element.12), channel_id=1, source_target_pairs={{1,0},{2,1},{3,2},{4,3},{5,4},{6,5},{7,6},{8,7},{9,8},{10,9},{11,1... | collective-permute-start | bytes 1179656 | tf_op jit(solution)/shard_map/ppermute | solution.py:416
  34.8 0.0 copy-done
  34.8 0.0 copy-done.4
  34.8 0.0 copy-done.3
  34.8 0.0 copy-done.2
  34.8 0.0 copy-start.1
  34.9 1.5 %copy-done.1 = f32[200,2304]{1,0:T(8,128)S(1)} copy-done((f32[200,2304]{1,0:T(8,128)S(1)}, f32[200,2304]{1,0:T(8,128)}, u32[]{:S(2)}) %copy-start.1) | copy-done | bytes 1843224
  36.3 0.0 copy-start.5
  36.4 0.8 %copy-done.5 = s32[64,128]{1,0:T(8,128)S(1)} copy-done((s32[64,128]{1,0:T(8,128)S(1)}, s32[64,128]{1,0:T(8,128)}, u32[]{:S(2)}) %copy-start.5) | copy-done | bytes 32792
  37.1 8.3 %sums.1 = (f32[188,8192]{1,0:T(8,128)S(1)}, f32[384,256]{1,0:T(8,128)S(1)}) custom-call(s32[64,128]{1,0:T(8,128)S(1)} %copy-done.5, f32[188,8192]{1,0:T(8,128)S(1)} %copy-done, f32[200,2304]{1,0:T(8,128)S(1)} %copy-done.1, f32[1,8192]{1,0:T(1,128)S(1)} %bitcast.19, s32[1,8192]{1,0:T(1,128)S(1)} %bitcast.16, s32[1,8192]{1,0:T(1,128)S(1)} %bitcast.13), custom_call_target="tpu_custom_call" | custom-call | flops 1610612736 | bytes 12320768 | tf_op jit(solution)/shard_map/sums/pallas_call | solution.py:422
  45.4 0.0 collective-permute-done.below
  45.4 0.0 collective-permute-done.1.above
  45.4 0.0 copy-done.6
  45.4 7.5 %mix.1 = (f32[188,9216]{1,0:T(8,128)}, f32[188,256]{1,0:T(8,128)}) custom-call(f32[188,8192]{1,0:T(8,128)S(1)} %get-tuple-element.10.reacted, s32[1,8192]{1,0:T(1,128)S(1)} %bitcast.17, s32[1,8192]{1,0:T(1,128)S(1)} %bitcast.14, f32[192,512]{1,0:T(8,128)S(1)} %collective-permute-done.below, f32[192,512]{1,0:T(8,128)S(1)} %collective-permute-done.1.above, ...), custom_call_target="tpu_custom_call" | custom-call | tf_op jit(solution)/shard_map/mix/pallas_call | solution.py:436
Async XLA Ops:
  0.6 34.2 %copy-start = (f32[188,8192]{1,0:T(8,128)S(1)}, f32[188,8192]{1,0:T(8,128)}, u32[]{:S(2)}) copy-start(f32[188,8192]{1,0:T(8,128)} %states.3) | copy-start | bytes 18481156
  0.6 34.2 %copy-start.4 = (f32[8192]{0:T(1024)S(1)}, f32[8192]{0:T(1024)}, u32[]{:S(2)}) copy-start(f32[8192]{0:T(1024)} %param.12) | copy-start | bytes 98308
  0.7 34.2 %copy-start.3 = (s32[8192]{0:T(1024)S(1)}, s32[8192]{0:T(1024)}, u32[]{:S(2)}) copy-start(s32[8192]{0:T(1024)} %param.14) | copy-start | bytes 98308
  0.7 34.2 %copy-start.2 = (s32[8192]{0:T(1024)S(1)}, s32[8192]{0:T(1024)}, u32[]{:S(2)}) copy-start(s32[8192]{0:T(1024)} %param.15) | copy-start | bytes 98308
  0.7 44.7 %copy-start.6 = (f32[256]{0:T(256)S(1)}, f32[256]{0:T(256)}, u32[]{:S(2)}) copy-start(f32[256]{0:T(256)} %param.21) | copy-start | bytes 3076
  27.4 18.0 %collective-permute-start = (f32[192,512]{1,0:T(8,128)}, f32[192,512]{1,0:T(8,128)S(1)}, u32[]{:S(2)}, u32[]{:S(2)}) collective-permute-start(f32[192,512]{1,0:T(8,128)} %get-tuple-element.11), channel_id=1, source_target_pairs={{0,1},{1,2},{2,3},{3,4},{4,5},{5,6},{6,7},{7,8},{8,9},{9,10},{10,1... | collective-permute-start | bytes 1179656 | tf_op jit(solution)/shard_map/ppermute | solution.py:415
  29.4 16.0 %collective-permute-start.1 = (f32[192,512]{1,0:T(8,128)}, f32[192,512]{1,0:T(8,128)S(1)}, u32[]{:S(2)}, u32[]{:S(2)}) collective-permute-start(f32[192,512]{1,0:T(8,128)} %get-tuple-element.12), channel_id=1, source_target_pairs={{1,0},{2,1},{3,2},{4,3},{5,4},{6,5},{7,6},{8,7},{9,8},{10,9},{11,1... | collective-permute-start | bytes 1179656 | tf_op jit(solution)/shard_map/ppermute | solution.py:416
  34.8 1.5 %copy-start.1 = (f32[200,2304]{1,0:T(8,128)S(1)}, f32[200,2304]{1,0:T(8,128)}, u32[]{:S(2)}) copy-start(f32[200,2304]{1,0:T(8,128)} %get-tuple-element.9.solved) | copy-start | bytes 5529604
  36.3 0.8 %copy-start.5 = (s32[64,128]{1,0:T(8,128)S(1)}, s32[64,128]{1,0:T(8,128)}, u32[]{:S(2)}) copy-start(s32[64,128]{1,0:T(8,128)} %get-tuple-element.8.base) | copy-start | bytes 98308
